TPU v7x, 32 devices: a whole 2x2x4 slice. The times are simulated.
32 devices in a mesh: centre: 8 (over z, y), row: 4 (over x, core).
Axes of the slice: x: 2, y: 2, z: 4, core: 2. Of those that a mesh axis runs over, the one named last changes fastest.
Arguments:
- pool: bfloat16 [1024, 16384], P('centre', 'row')
- batch_index: int32 [1024], P('row'), may hold values from 0 to 16383, as said below
- targets: float32 [10, 1024], P(None, 'row'), may hold values from -6 to 6
- centres: bfloat16 [65536, 1024], P(('centre', 'row'))
- weights: float32 [10, 65536], P(None, ('centre', 'row')), may hold values from -0.0234375 to 0.0234375
- sample_index: int32 [512], P(('centre', 'row')), may hold values from 0 to 65535, as said below
- factor: float32 [512, 128], P(('centre', 'row')), may hold values from -0.5 to 0.5
Outputs:
- gradient: float32 [10, 1024], P(None, 'row')
- update: float32 [10, 512], P(None, ('centre', 'row'))
Inputs may be any that keep to these rules, and one draw needn't show every extreme that they name: `batch_index`: the entries at positions r * 256 to (r + 1) * 256 - 1 lie in r * 4096 to (r + 1) * 4096 - 1; repeats may occur. `sample_index`: all entries differ; the entries at positions k * 16 to (k + 1) * 16 - 1 lie in k * 2048 to (k + 1) * 2048 - 1.
All inputs are finite; a program needn't handle non-finite values.
Results may differ from a plain program's by a relative error of at most 0.0003.
Values may be sent and summed in bfloat16 or wider, within the bound.
A program may use at most 128 MiB of HBM per device.

v0:
```python
import math
import jax
import jax.numpy as jnp
from jax import lax
from jax.sharding import PartitionSpec as P

PROJ_STEPS = 2
EPS = 1e-06
HIGH = lax.Precision.HIGHEST


def row_scale(rows, axis):
    values = rows.astype(jnp.float32)
    return jnp.sqrt(jnp.mean(values * values, axis=axis) + EPS)


def tangent_kernel(inner, left_scale, right_scale, width):
    product = left_scale[:, None] * right_scale[None, :]
    cosine = jnp.clip(inner / (width * product), -1.0, 1.0)
    angle = jnp.arccos(cosine)
    first = (math.pi - angle) / math.pi
    second = (cosine * (math.pi - angle) + jnp.sqrt(1.0 - cosine * cosine)) / math.pi
    return product * (second + cosine * first)


def on_device(pool, batch_index, targets, centres, weights, sample_index, factor):
    width = float(centres.shape[1])
    labels = weights.shape[0]
    rows_dev = batch_index.shape[0]
    pool_dev = pool.shape[1]
    cent_dev = centres.shape[0]
    samp_dev = sample_index.shape[0]
    row_count = lax.axis_size("row")
    total_rows = rows_dev * row_count
    total_samp = samp_dev * row_count * lax.axis_size("centre")
    contract = (((1,), (1,)), ((), ()))
    local_batch = batch_index - lax.axis_index("row") * pool_dev
    picked = jnp.take(pool, local_batch, axis=1)
    features = lax.all_gather(picked, "centre", axis=0, tiled=True)
    all_targets = lax.all_gather(targets, "row", axis=1, tiled=True)
    centre_scale = row_scale(centres, 1)
    local_sample = sample_index - lax.axis_index(("centre", "row")) * cent_dev
    sample_rows = jnp.take(centres, local_sample, axis=0)
    sample_scale = jnp.take(centre_scale, local_sample)
    piece = lax.all_gather(features, "row", axis=1, tiled=True)
    inner = jnp.dot(centres, piece, preferred_element_type=jnp.float32)
    kernel = tangent_kernel(inner, centre_scale, row_scale(piece, 0), width)
    partial_value = jnp.dot(weights, kernel, precision=HIGH)
    tiles = jnp.concatenate([partial_value, jnp.take(kernel, local_sample, axis=0)], axis=0)
    partial_value = tiles[:labels]
    cross = tiles[labels:]
    totals = lax.psum(partial_value, ("centre", "row"))
    gradient_all = totals - all_targets
    gradient = lax.dynamic_slice_in_dim(gradient_all, lax.axis_index("row") * rows_dev, rows_dev, 1)
    push = lax.dot_general(gradient_all, cross, contract, precision=HIGH) / total_rows
    piece = lax.all_gather(sample_rows, ("centre", "row"), axis=0, tiled=True)
    inner = lax.dot_general(sample_rows, piece, contract, preferred_element_type=jnp.float32)
    block = tangent_kernel(inner, sample_scale, row_scale(piece, 1), width)
    update = jnp.zeros((labels, samp_dev), jnp.float32)
    for step in range(PROJ_STEPS):
        if step == 0:
            slope = push
        else:
            update_whole = lax.all_gather(update, ("centre", "row"), axis=1, tiled=True)
            slope = (
                lax.dot_general(update_whole, block, contract, precision=HIGH) / total_samp + push
            )
        coef = lax.psum(jnp.dot(slope, factor, precision=HIGH), ("centre", "row"))
        update = update - (slope - jnp.dot(coef, factor.T, precision=HIGH))
    return (gradient, update)


def solution(mesh):
    placed = (
        P("centre", "row"),
        P("row"),
        P(None, "row"),
        P(("centre", "row"), None),
        P(None, ("centre", "row")),
        P(("centre", "row")),
        P(("centre", "row"), None),
    )
    return jax.shard_map(
        on_device,
        mesh=mesh,
        in_specs=placed,
        out_specs=(P(None, "row"), P(None, ("centre", "row"))),
        check_vma=False,
    )
```

profile of v0, /device:TPU:10, one launch (start us, length us, event | category | flops | bytes accessed | tf_op | source)
XLA Modules:
  0.0 314.5 jit_solution(3120540883913514165)
XLA Ops:
  7.2 0.0 copy-start
  7.2 0.0 copy-start.3
  7.2 0.0 all-gather.5.cloned.1.call-start
  7.2 0.7 compare_and_fusion
  7.9 3.3 %gather_fusion.3 = bf16[16,1024]{1,0:T(8,128)(2,1)S(1)} fusion(bf16[2048,1024]{1,0:T(8,128)(2,1)} %param.10, s32[1024]{0:T(1024)S(1)} %pad_clamp_fusion), kind=kCustom, calls=%fused_computation.3 | custom fusion | bytes 65600 | tf_op jit(solution)/shard_map/jit(_take)/gather | solution.py:43
  11.3 0.7 broadcast_select_fusion
  11.9 0.0 copy-start.1
  11.9 0.0 all-gather.5.cloned.1.call-update
  12.0 0.0 all-gather.3.cloned.1.call-start
  12.0 1.6 copy.13
  13.6 0.7 compare_and_fusion.1
  14.3 0.9 gather_fusion
  15.2 0.1 select_bitcast_fusion
  15.3 28.9 %all_gather.15 = bf16[1024,256]{0,1:T(8,128)(2,1)} all-gather(bf16[128,256]{0,1:T(8,128)(2,1)S(1)} %select_bitcast_fusion), channel_id=1, replica_groups=mesh['centre'=8,'row'=4] {'centre'}, dimensions={0}, use_global_device_ids=true | all-gather | bytes 589824 | tf_op jit(solution)/shard_map/all_gather | solution.py:39
  44.2 0.0 all-gather.3.cloned.1.call-update
  44.2 3.1 multiply_reduce_fusion
  47.3 0.7 gather_fusion.2
  48.0 0.0 copy-done.3
  48.0 5.2 %all_gather.17 = f32[10,1024]{1,0:T(8,128)S(1)} all-gather(f32[10,256]{1,0:T(8,128)S(1)} %copy-done.3), channel_id=1, replica_groups=mesh['centre'=8,'row'=4] {'row'}, dimensions={1}, use_global_device_ids=true | all-gather | bytes 51200 | tf_op jit(solution)/shard_map/all_gather | solution.py:40
  53.2 13.0 %all-gather.5.cloned.1.call-done = bf16[512,1024]{1,0:T(8,128)(2,1)} async-done(((bf16[16,1024]{1,0:T(8,128)(2,1)}), bf16[512,1024]{1,0:T(8,128)(2,1)}) %all-gather.5.cloned.1.call-update) | async-done | bytes 1048592 | tf_op jit(solution)/shard_map/all_gather | solution.py:56
  66.3 1.5 multiply_reduce_fusion.2
  67.8 0.0 copy-done.1
  67.8 1.6 fusion.2
  69.4 19.9 %all-gather.3.cloned.1.call-done = bf16[1024,1024]{0,1:T(8,128)(2,1)} async-done(((bf16[1024,256]{0,1:T(8,128)(2,1)}), bf16[1024,1024]{0,1:T(8,128)(2,1)}) %all-gather.3.cloned.1.call-update) | async-done | bytes 2097168 | tf_op jit(solution)/shard_map/all_gather | solution.py:45
  89.2 2.1 multiply_reduce_fusion.1
  91.3 29.4 %multiply_multiply_fusion = f32[2048,1024]{0,1:T(8,128)} fusion(bf16[1024,1024]{0,1:T(8,128)(2,1)} %all-gather.3.cloned.1.call-done, bf16[2048,1024]{1,0:T(8,128)(2,1)} %param.10, f32[1024]{0:T(1024)S(1)} %add_sqrt_fusion.1, f32[2048]{0:T(1024)S(1)} %add_sqrt_fusion), kind=kOutput, calls=%fused_computation.4 | convolution fusion | flops 4330618880 | bytes 14692352 | tf_op jit(solution)/shard_map/dot_general | solution.py:46
  120.7 9.3 %copy.14 = f32[2048,1024]{1,0:T(8,128)} copy(f32[2048,1024]{0,1:T(8,128)} %multiply_multiply_fusion) | data formatting | bytes 16777216 | tf_op jit(solution)/shard_map/mul | solution.py:23
  129.9 0.0 copy-start.2
  129.9 4.0 %gather_fusion.1 = f32[16,1024]{1,0:T(8,128)S(1)} fusion(f32[2048,1024]{1,0:T(8,128)} %copy.14, s32[1024]{0:T(1024)S(1)} %pad_clamp_fusion), kind=kCustom, calls=%fused_computation.1 | custom fusion | bytes 131136 | tf_op jit(solution)/shard_map/jit(_take)/gather | solution.py:49
  134.0 0.0 copy-done
  134.0 9.4 %convolution_bitcast_fusion = f32[10,1024]{1,0:T(8,128)S(1)} fusion(f32[2048,1024]{0,1:T(8,128)} %multiply_multiply_fusion, f32[10,2048]{1,0:T(8,128)S(1)} %copy-done), kind=kOutput, calls=%fused_computation.11 | convolution fusion | flops 251658240 | bytes 8511488 | tf_op jit(solution)/shard_map/dot_general | solution.py:48
  143.4 41.3 %psum.21 = f32[10,1024]{1,0:T(8,128)S(1)} all-reduce(f32[10,1024]{1,0:T(8,128)S(1)} %convolution_bitcast_fusion), channel_id=1, replica_groups=mesh['centre'=8,'row'=4] {'centre','row'}, use_global_device_ids=true, to_apply=%region_2.3 | all-reduce | flops 10240 | bytes 81920 | tf_op jit(solution)/shard_map/psum | solution.py:52
  184.7 0.2 convolution_multiply_fusion.1
  185.0 0.0 copy-done.2
  185.0 0.1 fusion.33
  185.1 40.0 %psum.22 = f32[10,128]{1,0:T(8,128)S(1)} all-reduce(f32[10,128]{1,0:T(8,128)S(1)} %fusion.33), channel_id=1, replica_groups=mesh['centre'=8,'row'=4] {'centre','row'}, use_global_device_ids=true, to_apply=%region_3.4 | all-reduce | flops 1280 | bytes 10240 | tf_op jit(solution)/shard_map/psum | solution.py:68
  225.2 0.1 fusion.5
  225.3 0.1 copy.15
  225.4 31.4 %all_gather.18 = f32[10,512]{0,1:T(8,128)S(1)} all-gather(f32[10,16]{0,1:T(8,128)S(1)} %copy.15), channel_id=1, replica_groups=mesh['centre'=8,'row'=4] {'centre','row'}, dimensions={1}, use_global_device_ids=true | all-gather | bytes 21120 | tf_op jit(solution)/shard_map/all_gather | solution.py:64
  256.8 0.6 fusion.4
  257.4 0.1 fusion.34
  257.5 48.8 %psum.23 = f32[10,128]{1,0:T(8,128)S(1)} all-reduce(f32[10,128]{1,0:T(8,128)S(1)} %fusion.34), channel_id=1, replica_groups=mesh['centre'=8,'row'=4] {'centre','row'}, use_global_device_ids=true, to_apply=%region_5.6 | all-reduce | flops 1280 | bytes 10240 | tf_op jit(solution)/shard_map/psum | solution.py:68
  306.4 0.7 fusion.3
  307.1 0.6 constant_dynamic-slice_fusion
  (7 shorter events, 0.1 us)
Async XLA Ops:
  7.2 126.8 %copy-start = (f32[10,2048]{1,0:T(8,128)S(1)}, f32[10,2048]{1,0:T(8,128)}, u32[]{:S(2)}) copy-start(f32[10,2048]{1,0:T(8,128)} %param.11) | copy-start | bytes 245764
  7.2 40.8 %copy-start.3 = (f32[10,256]{1,0:T(8,128)S(1)}, f32[10,256]{1,0:T(8,128)}, u32[]{:S(2)}) copy-start(f32[10,256]{1,0:T(8,128)} %param.9) | copy-start | bytes 30724
  7.2 59.1 %all-gather.5.cloned.1.call-start = ((), (), s32[]{:S(2)}) async-start(), calls=%async_computation.1 | async-start | bytes 1081344 | tf_op jit(solution)/shard_map/all_gather | solution.py:56
  11.9 55.8 %copy-start.1 = (bf16[16,1024]{1,0:T(8,128)(2,1)S(1)}, bf16[16,1024]{1,0:T(8,128)(2,1)}, u32[]{:S(2)}) copy-start(bf16[16,1024]{1,0:T(8,128)(2,1)} %broadcast_select_fusion) | copy-start | bytes 98308
  12.0 77.3 %all-gather.3.cloned.1.call-start = ((), (), s32[]{:S(2)}) async-start(), calls=%async_computation | async-start | bytes 2621440 | tf_op jit(solution)/shard_map/all_gather | solution.py:45
  129.9 55.0 %copy-start.2 = (f32[16,128]{1,0:T(8,128)S(1)}, f32[16,128]{1,0:T(8,128)}, u32[]{:S(2)}) copy-start(f32[16,128]{1,0:T(8,128)} %param.13) | copy-start | bytes 24580
Sparse Core Ops, SparseCore 0:
  12.1 54.1 all-gather.4
  67.8 21.3 all-gather.2
where the time goes:
time: 315 us
  blocking collectives  196 us (62%)
  matrix products  42.3 us (13%)
  waiting for transfers between devices  32.9 us (10%)
  local copies, waits for them, and re-layouts  20.5 us (7%)
  between operations  14.2 us (5%)
  other arithmetic  8.84 us (3%)
    psum x2, blocking collectives, on_device(): coef = lax.psum(jnp.dot(slope, factor, precision=HIGH), ('centre', 'row'))  88.9 us
    psum x1, blocking collectives, on_device(): totals = lax.psum(partial_value, ('centre', 'row'))  41.3 us
    all_gather x1, blocking collectives, on_device(): update_whole = lax.all_gather(update, ('centre', 'row'), axis=1, tiled=True)  31.4 us
    dot_general x1, matrix products, on_device(): inner = jnp.dot(centres, piece, preferred_element_type=jnp.float32)  29.4 us
    all_gather x1, blocking collectives, on_device(): features = lax.all_gather(picked, 'centre', axis=0, tiled=True)  28.9 us
    all_gather x1, waiting for transfers between devices, on_device(): piece = lax.all_gather(features, 'row', axis=1, tiled=True)  19.9 us
    all_gather x1, waiting for transfers between devices, on_device(): piece = lax.all_gather(sample_rows, ('centre', 'row'), axis=0, tiled=True)  13 us
    dot_general x1, matrix products, on_device(): partial_value = jnp.dot(weights, kernel, precision=HIGH)  9.43 us
  transfers between devices with their start and end apart: 2, of which 2 were waited for; matrix products, arithmetic and copies ran while one was open for 3% of the time, Pallas kernels for 0%

commit v1 on v0

--- a/solution.py
+++ b/solution.py
@@ -37,12 +37,17 @@
     local_batch = batch_index - lax.axis_index("row") * pool_dev
     picked = jnp.take(pool, local_batch, axis=1)
     features = lax.all_gather(picked, "centre", axis=0, tiled=True)
-    all_targets = lax.all_gather(targets, "row", axis=1, tiled=True)
     centre_scale = row_scale(centres, 1)
     local_sample = sample_index - lax.axis_index(("centre", "row")) * cent_dev
     sample_rows = jnp.take(centres, local_sample, axis=0)
     sample_scale = jnp.take(centre_scale, local_sample)
-    piece = lax.all_gather(features, "row", axis=1, tiled=True)
+    all_targets, piece = jnp.split(
+        lax.all_gather(
+            jnp.concatenate([targets, features], 0), axis_name="row", axis=1, tiled=True
+        ),
+        [targets.shape[0]],
+        0,
+    )
     inner = jnp.dot(centres, piece, preferred_element_type=jnp.float32)
     kernel = tangent_kernel(inner, centre_scale, row_scale(piece, 0), width)
     partial_value = jnp.dot(weights, kernel, precision=HIGH)

time: 315 us -> 330 us (1.048)
  waiting for transfers between devices: 32.9 us -> 48.2 us
  blocking collectives: 196 us -> 191 us
  other arithmetic: 8.84 us -> 12.2 us
    all_gather x1, waiting for transfers between devices: 19.9 us -> 32.2 us  [on_device(): lax.all_gather(jnp.concatenate([targets, features], 0), axis_name='row',...]
    all_gather x1 -> x0, blocking collectives: 5.25 us -> none  [on_device(): all_targets = lax.all_gather(targets, 'row', axis=1, tiled=True)]
  transfers between devices with their start and end apart: 2 -> 2, of which waited for: 2 -> 2; matrix products, arithmetic and copies ran while one was open for 3% -> 4% of each run, Pallas kernels for 0% -> 0%
where the time goes in v1:
time: 330 us; the launch traced here: 329 us
  blocking collectives  191 us (58%)
  waiting for transfers between devices  48.2 us (15%)
  matrix products  43.4 us (13%)
  local copies, waits for them, and re-layouts  20.6 us (6%)
  between operations  14.2 us (4%)
  other arithmetic  12.2 us (4%)
    psum x2, blocking collectives, on_device(): coef = lax.psum(jnp.dot(slope, factor, precision=HIGH), ('centre', 'row'))  89 us
    psum x1, blocking collectives, on_device(): totals = lax.psum(partial_value, ('centre', 'row'))  41.3 us
    all_gather x1, waiting for transfers between devices, on_device(): lax.all_gather(jnp.concatenate([targets, features], 0), axis_name='row',...  32.2 us
    all_gather x1, blocking collectives, on_device(): update_whole = lax.all_gather(update, ('centre', 'row'), axis=1, tiled=True)  31.4 us
    dot_general x1, matrix products, on_device(): inner = jnp.dot(centres, piece, preferred_element_type=jnp.float32)  30.4 us
    all_gather x1, blocking collectives, on_device(): features = lax.all_gather(picked, 'centre', axis=0, tiled=True)  29.2 us
    all_gather x1, waiting for transfers between devices, on_device(): piece = lax.all_gather(sample_rows, ('centre', 'row'), axis=0, tiled=True)  16 us
    dot_general x1, matrix products, on_device(): partial_value = jnp.dot(weights, kernel, precision=HIGH)  9.43 us
  transfers between devices with their start and end apart: 2, of which 2 were waited for; matrix products, arithmetic and copies ran while one was open for 4% of the time, Pallas kernels for 0%

profile of v1, /device:TPU:10, one launch (start us, length us, event | category | flops | bytes accessed | tf_op | source)
XLA Modules:
  0.0 329.5 jit_solution(9459336118811070634)
XLA Ops:
  7.2 0.0 copy-start
  7.2 0.0 all-gather.5.cloned.1.call-start
  7.2 0.7 compare_and_fusion
  7.9 3.3 %gather_fusion.3 = bf16[16,1024]{1,0:T(8,128)(2,1)S(1)} fusion(bf16[2048,1024]{1,0:T(8,128)(2,1)} %param.10, s32[1024]{0:T(1024)S(1)} %pad_clamp_fusion), kind=kCustom, calls=%fused_computation.3 | custom fusion | bytes 65600 | tf_op jit(solution)/shard_map/jit(_take)/gather | solution.py:42
  11.3 0.7 broadcast_select_fusion
  11.9 0.0 copy-start.1
  11.9 0.0 all-gather.5.cloned.1.call-update
  12.0 0.0 all-gather.3.cloned.1.call-start
  12.0 1.6 copy.15
  13.6 0.7 compare_and_fusion.1
  14.3 0.9 gather_fusion
  15.2 0.1 copy.16
  15.3 29.2 %all_gather.12 = bf16[1024,256]{1,0:T(8,128)(2,1)S(1)} all-gather(bf16[128,256]{1,0:T(8,128)(2,1)S(1)} %select_bitcast_fusion), channel_id=1, replica_groups=mesh['centre'=8,'row'=4] {'centre'}, dimensions={0}, use_global_device_ids=true | all-gather | bytes 589824 | tf_op jit(solution)/shard_map/all_gather | solution.py:39
  44.6 0.1 convert_element_type.10
  44.6 1.8 pad_maximum_fusion
  46.4 0.0 all-gather.3.cloned.1.call-update
  46.4 3.1 multiply_reduce_fusion
  49.5 0.7 gather_fusion.2
  50.2 16.0 %all-gather.5.cloned.1.call-done = bf16[512,1024]{1,0:T(8,128)(2,1)} async-done(((bf16[16,1024]{1,0:T(8,128)(2,1)}), bf16[512,1024]{1,0:T(8,128)(2,1)}) %all-gather.5.cloned.1.call-update) | async-done | bytes 1048592 | tf_op jit(solution)/shard_map/all_gather | solution.py:61
  66.2 1.5 multiply_reduce_fusion.2
  67.7 0.0 copy-done.1
  67.7 1.6 fusion.3
  69.3 32.2 %all-gather.3.cloned.1.call-done = f32[1034,1024]{1,0:T(8,128)} async-done(((f32[1034,256]{1,0:T(8,128)}), f32[1034,1024]{1,0:T(8,128)}) %all-gather.3.cloned.1.call-update) | async-done | bytes 4235280 | tf_op jit(solution)/shard_map/all_gather | solution.py:45
  101.5 2.8 multiply_reduce_fusion.1
  104.3 30.4 %multiply_multiply_fusion = f32[2048,1024]{0,1:T(8,128)} fusion(bf16[2048,1024]{1,0:T(8,128)(2,1)} %param.10, f32[1024]{0:T(1024)S(1)} %add_sqrt_fusion.1, f32[2048]{0:T(1024)S(1)} %add_sqrt_fusion, f32[1034,1024]{1,0:T(8,128)} %all-gather.3.cloned.1.call-done), kind=kOutput, calls=%fused_computation.4 | convolution fusion | flops 4330618880 | bytes 14692352 | tf_op jit(solution)/shard_map/dot_general | solution.py:51
  134.7 9.3 %copy.17 = f32[2048,1024]{1,0:T(8,128)} copy(f32[2048,1024]{0,1:T(8,128)} %multiply_multiply_fusion) | data formatting | bytes 16777216 | tf_op jit(solution)/shard_map/mul | solution.py:23
  144.0 0.0 copy-done
  144.0 0.0 copy-start.2
  144.0 9.4 %convolution_bitcast_fusion = f32[10,1024]{1,0:T(8,128)S(1)} fusion(f32[2048,1024]{0,1:T(8,128)} %multiply_multiply_fusion, f32[10,2048]{1,0:T(8,128)S(1)} %copy-done), kind=kOutput, calls=%fused_computation.12 | convolution fusion | flops 251658240 | bytes 8511488 | tf_op jit(solution)/shard_map/dot_general | solution.py:53
  153.5 41.3 %psum.21 = f32[10,1024]{1,0:T(8,128)S(1)} all-reduce(f32[10,1024]{1,0:T(8,128)S(1)} %convolution_bitcast_fusion), channel_id=1, replica_groups=mesh['centre'=8,'row'=4] {'centre','row'}, use_global_device_ids=true, to_apply=%region_2.3 | all-reduce | flops 10240 | bytes 81920 | tf_op jit(solution)/shard_map/psum | solution.py:57
  194.8 4.0 %gather_fusion.1 = f32[16,1024]{1,0:T(8,128)S(1)} fusion(f32[2048,1024]{1,0:T(8,128)} %copy.17, s32[1024]{0:T(1024)S(1)} %pad_clamp_fusion), kind=kCustom, calls=%fused_computation.1 | custom fusion | bytes 131136 | tf_op jit(solution)/shard_map/jit(_take)/gather | solution.py:54
  198.8 0.8 slice_subtract_fusion
  199.6 0.2 convolution_multiply_fusion.1
  199.9 0.0 copy-done.2
  199.9 0.1 fusion.34
  200.0 40.1 %psum.22 = f32[10,128]{1,0:T(8,128)S(1)} all-reduce(f32[10,128]{1,0:T(8,128)S(1)} %fusion.34), channel_id=1, replica_groups=mesh['centre'=8,'row'=4] {'centre','row'}, use_global_device_ids=true, to_apply=%region_3.4 | all-reduce | flops 1280 | bytes 10240 | tf_op jit(solution)/shard_map/psum | solution.py:73
  240.2 0.1 fusion.6
  240.3 0.1 copy.18
  240.4 31.4 %all_gather.14 = f32[10,512]{0,1:T(8,128)S(1)} all-gather(f32[10,16]{0,1:T(8,128)S(1)} %copy.18), channel_id=1, replica_groups=mesh['centre'=8,'row'=4] {'centre','row'}, dimensions={1}, use_global_device_ids=true | all-gather | bytes 21120 | tf_op jit(solution)/shard_map/all_gather | solution.py:69
  271.7 0.6 fusion.5
  272.3 0.1 fusion.35
  272.4 48.9 %psum.23 = f32[10,128]{1,0:T(8,128)S(1)} all-reduce(f32[10,128]{1,0:T(8,128)S(1)} %fusion.35), channel_id=1, replica_groups=mesh['centre'=8,'row'=4] {'centre','row'}, use_global_device_ids=true, to_apply=%region_5.6 | all-reduce | flops 1280 | bytes 10240 | tf_op jit(solution)/shard_map/psum | solution.py:73
  321.3 0.7 fusion.4
  322.0 0.6 constant_dynamic-slice_fusion
  (7 shorter events, 0.1 us)
Async XLA Ops:
  7.2 136.9 %copy-start = (f32[10,2048]{1,0:T(8,128)S(1)}, f32[10,2048]{1,0:T(8,128)}, u32[]{:S(2)}) copy-start(f32[10,2048]{1,0:T(8,128)} %param.11) | copy-start | bytes 245764
  7.2 59.0 %all-gather.5.cloned.1.call-start = ((), (), s32[]{:S(2)}) async-start(), calls=%async_computation.1 | async-start | bytes 1081344 | tf_op jit(solution)/shard_map/all_gather | solution.py:61
  11.9 55.8 %copy-start.1 = (bf16[16,1024]{1,0:T(8,128)(2,1)S(1)}, bf16[16,1024]{1,0:T(8,128)(2,1)}, u32[]{:S(2)}) copy-start(bf16[16,1024]{1,0:T(8,128)(2,1)} %broadcast_select_fusion) | copy-start | bytes 98308
  12.0 89.5 %all-gather.3.cloned.1.call-start = ((), (), s32[]{:S(2)}) async-start(), calls=%async_computation | async-start | bytes 5324800 | tf_op jit(solution)/shard_map/all_gather | solution.py:45
  144.0 55.9 %copy-start.2 = (f32[16,128]{1,0:T(8,128)S(1)}, f32[16,128]{1,0:T(8,128)}, u32[]{:S(2)}) copy-start(f32[16,128]{1,0:T(8,128)} %param.13) | copy-start | bytes 24580
Sparse Core Ops, SparseCore 0:
  12.1 54.0 all-gather.4
  67.8 33.7 all-gather.2
